TPU v7x, 32 devices: a whole 2x2x4 slice. The times are simulated.
32 devices in a mesh: rows: 16 (over z, y, x), feat: 2 (over core).
Axes of the slice: x: 2, y: 2, z: 4, core: 2. Of those that a mesh axis runs over, the one named last changes fastest.
Arguments:
- score: float32 [32768, 128], P('rows', 'feat'), may hold values from -4 to 4
- event: int32 [32768, 128], P('rows', 'feat'), may hold values 0 or 1
- leaf: int32 [32768, 128], P('rows', 'feat'), may hold values from 0 to 1
- bins: int32 [32768, 256], P('rows'), may hold values from 0 to 31
- split_feature: int32 [128], P('feat'), may hold values from 0 to 255
- split_bin: int32 [128], P('feat'), may hold values from 0 to 30
Outputs:
- grad_hist: float32 [256, 32, 2, 128], P(('rows', 'feat'))
- hess_hist: float32 [256, 32, 2, 128], P(('rows', 'feat'))
- new_leaf: int32 [32768, 128], P('rows', 'feat')
All inputs are finite; a program needn't handle non-finite values. No bound on the sum of `event` on one device may be relied on, other than what follows from the above.
Results may differ from a plain program's by a relative error of at most 0.0026.
Values may be sent and summed in bfloat16 or wider, within the bound.
A program may use at most 64 MiB of HBM per device.

v0:
```python
import jax
import jax.numpy as jnp
from jax import lax
from jax.sharding import PartitionSpec as P

BINS = 32
LEAVES = 2


def histogram(columns, weight_matrix):
    row_count, col_count = columns.shape
    block_rows = min(row_count, 512)
    levels = jnp.arange(BINS, dtype=jnp.int32)

    def hist_step(turn_index, running):
        column_piece = lax.dynamic_slice_in_dim(columns, turn_index * block_rows, block_rows, 0)
        weight_rows = lax.dynamic_slice_in_dim(
            weight_matrix, turn_index * block_rows, block_rows, 0
        )
        onehot = (
            (column_piece[:, :, None] == levels)
            .reshape(block_rows, col_count * BINS)
            .astype(jnp.bfloat16)
        )
        return running + lax.dot_general(
            onehot, weight_rows, (((0,), (0,)), ((), ())), preferred_element_type=jnp.float32
        )

    zeros_init = jnp.zeros((col_count * BINS, weight_matrix.shape[1]), jnp.float32)
    return lax.fori_loop(0, row_count // block_rows, hist_step, zeros_init)


def per_device(score, event, leaf, bins, split_feature, split_bin):
    row_count = score.shape[0]
    shard_count = lax.axis_size("rows")
    own_index = lax.axis_index("rows")
    exp_score = jnp.exp(score)
    event_mass = event.astype(jnp.float32)
    local_suffix = lax.cumsum(exp_score, axis=0, reverse=True)
    risk_total = local_suffix[0]
    shard_ids = jnp.arange(shard_count, dtype=jnp.int32)
    every_total = lax.all_gather(risk_total[None, :], "rows", axis=0, tiled=True)
    is_later = (shard_ids > own_index)[:, None]
    later_sum = jnp.sum(jnp.where(is_later, every_total, jnp.zeros((), jnp.float32)), axis=0)
    risk_sum = local_suffix + later_sum
    event_share = event_mass / risk_sum
    local_hazard = jnp.cumsum(event_share, axis=0)
    local_square = jnp.cumsum(event_share / risk_sum, axis=0)
    hazard_total = local_hazard[-1]
    square_total = local_square[-1]
    every_hazard, every_square = (
        lax.all_gather(hazard_total[None, :], "rows", axis=0, tiled=True),
        lax.all_gather(square_total[None, :], "rows", axis=0, tiled=True),
    )
    is_earlier = (shard_ids < own_index)[:, None]
    earlier_hazard = jnp.sum(
        jnp.where(is_earlier, every_hazard, jnp.zeros((), jnp.float32)), axis=0
    )
    earlier_square = jnp.sum(
        jnp.where(is_earlier, every_square, jnp.zeros((), jnp.float32)), axis=0
    )
    cum_hazard = local_hazard + earlier_hazard
    cum_square = local_square + earlier_square
    scale_factor = BINS * LEAVES / (row_count * shard_count)
    gradient = scale_factor * (exp_score * cum_hazard - event_mass)
    hessian = scale_factor * (exp_score * cum_hazard - exp_score * exp_score * cum_square)
    in_leaf = leaf[:, None, :] == jnp.arange(LEAVES, dtype=jnp.int32)[None, :, None]
    leaf_weights = jnp.stack(
        [
            jnp.where(in_leaf, gradient[:, None, :], jnp.zeros((), jnp.float32)),
            jnp.where(in_leaf, hessian[:, None, :], jnp.zeros((), jnp.float32)),
        ],
        axis=1,
    ).astype(jnp.bfloat16)
    split_value = jnp.take(bins, split_feature, axis=1)
    new_leaf = 2 * leaf + (split_value > split_bin[None, :]).astype(jnp.int32)
    feat_count = lax.axis_size("feat")
    feat_index = lax.axis_index("feat")
    everyone = lax.all_gather(leaf_weights, "feat", axis=3, tiled=True)
    weight_matrix = everyone.reshape(row_count, -1)
    per_owner = bins.shape[1] // (shard_count * feat_count)
    grouped = bins.reshape(row_count, shard_count, feat_count, per_owner)
    owned_columns = lax.dynamic_index_in_dim(grouped, feat_index, 2, keepdims=False).reshape(
        row_count, shard_count * per_owner
    )
    summed = lax.psum_scatter(
        histogram(owned_columns, weight_matrix).reshape(
            lax.axis_size("rows") * per_owner, BINS, 2, LEAVES, -1
        ),
        "rows",
        scatter_dimension=0,
        tiled=True,
    )
    return (summed[:, :, 0], summed[:, :, 1], new_leaf)


def solution(mesh):
    return jax.shard_map(
        per_device,
        mesh=mesh,
        in_specs=(
            P("rows", "feat"),
            P("rows", "feat"),
            P("rows", "feat"),
            P("rows", None),
            P("feat"),
            P("feat"),
        ),
        out_specs=(
            P(("rows", "feat"), None, None, None),
            P(("rows", "feat"), None, None, None),
            P("rows", "feat"),
        ),
        check_vma=False,
    )
```

profile of v0, /device:TPU:0, one launch (start us, length us, event | category | flops | bytes accessed | tf_op | source)
XLA Modules:
  0.0 507.1 jit_solution(16986218636305102861)
XLA Ops:
  7.2 1.1 exponential_bitcast_fusion
  8.5 79.3 %reduce-window.20 = f32[64,16,128]{2,1,0:T(8,128)S(1)} reduce-window(f32[64,16,128]{2,1,0:T(8,128)S(1)} %bitcast.94, f32[]{:T(128)} %constant.62.clone.1), window={size=1x1x128 pad=0_0x0_0x0_127}, to_apply=%region_0.0 | reduce-window | flops 16646144 | bytes 1048580 | tf_op jit(solution)/shard_map/reduce-window
  89.0 42.2 %all-gather = f32[16,1,64]{2,1,0:T(1,128)S(1)} all-gather(f32[1,1,64]{2,1,0:T(1,128)S(1)} %bitcast.108), channel_id=1, replica_groups=mesh['rows'=16,'feat'=2] {'rows'}, dimensions={0}, use_global_device_ids=true | all-gather | bytes 4352 | tf_op jit(solution)/shard_map/all_gather | solution.py:42
  131.8 18.1 %reduce-window.26 = f32[64,16,128]{2,1,0:T(8,128)S(1)} reduce-window(f32[64,16,128]{2,1,0:T(8,128)S(1)} %bitcast.95, f32[]{:T(128)} %constant.62.clone.1), window={size=1x1x128 pad=0_0x0_0x127_0}, to_apply=%region_6.7 | reduce-window | flops 16646144 | bytes 1048580 | tf_op jit(solution)/shard_map/reduce-window.4
  151.3 35.3 %all-gather.2 = f32[16,1,64]{2,1,0:T(1,128)S(1)} all-gather(f32[1,1,64]{2,1,0:T(1,128)S(1)} %bitcast.109), channel_id=1, replica_groups=mesh['rows'=16,'feat'=2] {'rows'}, dimensions={0}, use_global_device_ids=true | all-gather | bytes 4352 | tf_op jit(solution)/shard_map/all_gather | solution.py:53
  186.6 18.1 %reduce-window.24 = f32[64,16,128]{2,1,0:T(8,128)S(1)} reduce-window(f32[64,16,128]{2,1,0:T(8,128)S(1)} %bitcast.96, f32[]{:T(128)} %constant.62.clone.1), window={size=1x1x128 pad=0_0x0_0x127_0}, to_apply=%region_3.4 | reduce-window | flops 16646144 | bytes 1048580 | tf_op jit(solution)/shard_map/reduce-window.2
  206.2 37.3 %all-gather.1 = f32[16,1,64]{2,1,0:T(1,128)S(1)} all-gather(f32[1,1,64]{2,1,0:T(1,128)S(1)} %bitcast.110), channel_id=1, replica_groups=mesh['rows'=16,'feat'=2] {'rows'}, dimensions={0}, use_global_device_ids=true | all-gather | bytes 4352 | tf_op jit(solution)/shard_map/all_gather | solution.py:52
  245.1 2.4 pad_maximum_fusion
  247.9 1.9 copy.40
  249.9 4.3 all-gather.5.cloned.1.call-done
  254.2 4.1 copy.47
  258.3 41.4 %while.14 = (s32[]{:T(128)}, f32[4096,512]{1,0:T(8,128)}, s32[2048,128]{0,1:T(8,128)S(1)}, bf16[2048,512]{0,1:T(8,128)(2,1)}, s32[]{:T(128)}, /*index=5*/s32[]{:T(128)}, s32[]{:T(128)}, s32[]{:T(128)}) while((s32[]{:T(128)}, f32[4096,512]{1,0:T(8,128)}, s32[2048,128]{0,1:T(8,128)S(1)}, bf16[2048,512]{0,1:T(8,128)(2,1)}, ...), condition=%wide.region_10.11_spmd.clone, body=%wide.region_9.10_spmd.clone.sunk | while | flops 2153775104 | bytes 22347932 | solution.py:30
  258.5 1.5 bitcast_compare_fusion.2
  260.0 6.8 %select_add_fusion.2 = f32[4096,512]{1,0:T(8,128)} fusion(f32[4096,512]{1,0:T(8,128)} %get-tuple-element.177, pred[512,4096]{0,1:T(32,128)(4,1)S(1)} %bitcast_compare_fusion.2, pred[]{:T(512)S(6)} %compare.3, bf16[2048,512]{0,1:T(8,128)(2,1)} %get-tuple-element.187, s32[]{:T(128)S(6)} %select_n.74), kind=kOutput, calls=%fused_computation.3.clone.1 | convolution fusion | flops 2151677952 | bytes 19398660 | tf_op jit(solution)/shard_map/while/body/eval_jaxpr/dot_general | solution.py:25
  266.9 1.5 bitcast_compare_fusion.2
  268.4 9.3 %select_add_fusion.2 = f32[4096,512]{1,0:T(8,128)} fusion(f32[4096,512]{1,0:T(8,128)} %get-tuple-element.177, pred[512,4096]{0,1:T(32,128)(4,1)S(1)} %bitcast_compare_fusion.2, pred[]{:T(512)S(6)} %compare.3, bf16[2048,512]{0,1:T(8,128)(2,1)} %get-tuple-element.187, s32[]{:T(128)S(6)} %select_n.74), kind=kOutput, calls=%fused_computation.3.clone.1 | convolution fusion | flops 2151677952 | bytes 19398660 | tf_op jit(solution)/shard_map/while/body/eval_jaxpr/dot_general | solution.py:25
  277.9 1.5 bitcast_compare_fusion.2
  279.4 9.4 %select_add_fusion.2 = f32[4096,512]{1,0:T(8,128)} fusion(f32[4096,512]{1,0:T(8,128)} %get-tuple-element.177, pred[512,4096]{0,1:T(32,128)(4,1)S(1)} %bitcast_compare_fusion.2, pred[]{:T(512)S(6)} %compare.3, bf16[2048,512]{0,1:T(8,128)(2,1)} %get-tuple-element.187, s32[]{:T(128)S(6)} %select_n.74), kind=kOutput, calls=%fused_computation.3.clone.1 | convolution fusion | flops 2151677952 | bytes 19398660 | tf_op jit(solution)/shard_map/while/body/eval_jaxpr/dot_general | solution.py:25
  288.9 1.5 bitcast_compare_fusion.2
  290.4 9.4 %select_add_fusion.2 = f32[4096,512]{1,0:T(8,128)} fusion(f32[4096,512]{1,0:T(8,128)} %get-tuple-element.177, pred[512,4096]{0,1:T(32,128)(4,1)S(1)} %bitcast_compare_fusion.2, pred[]{:T(512)S(6)} %compare.3, bf16[2048,512]{0,1:T(8,128)(2,1)} %get-tuple-element.187, s32[]{:T(128)S(6)} %select_n.74), kind=kOutput, calls=%fused_computation.3.clone.1 | convolution fusion | flops 2151677952 | bytes 19398660 | tf_op jit(solution)/shard_map/while/body/eval_jaxpr/dot_general | solution.py:25
  299.7 10.6 %reshape.101 = f32[128,32,2,2,128]{4,3,2,1,0:T(2,128)} reshape(f32[4096,512]{1,0:T(8,128)} %get-tuple-element.97) | data formatting | bytes 16777216 | tf_op jit(solution)/shard_map/reshape | solution.py:87
  310.3 7.9 %copy.49 = f32[128,32,2,2,128]{4,1,3,2,0:T(8,128)} copy(f32[128,32,2,2,128]{4,3,2,1,0:T(2,128)} %reshape.101) | data formatting | bytes 16777216 | tf_op jit(solution)/shard_map/reshape | solution.py:87
  320.9 176.4 %reduce-scatter.2.cloned.1.call-done = f32[8,32,2,2,128]{4,1,3,2,0:T(8,128)} async-done(((f32[128,32,2,2,128]{4,1,3,2,0:T(8,128)}), f32[8,32,2,2,128]{4,1,3,2,0:T(8,128)}) %reduce-scatter.2.cloned.1.call-update) | async-done | bytes 524304 | tf_op jit(solution)/shard_map/reduce_scatter | solution.py:86
  497.3 1.1 slice_bitcast_fusion
  (65 shorter events, 11.7 us)
Async XLA Ops:
  7.2 247.1 %all-gather.5.cloned.1.call-start = ((), (), s32[]{:S(2)}) async-start(), calls=%async_computation.1 | async-start | bytes 3145728 | tf_op jit(solution)/shard_map/all_gather | solution.py:79
  8.5 122.8 %copy-start = (s32[2048,64]{0,1:T(8,128)S(1)}, s32[2048,64]{0,1:T(8,128)}, u32[]{:S(2)}) copy-start(s32[2048,64]{0,1:T(8,128)} %param.9) | copy-start | bytes 1572868
  204.8 38.8 %copy-start.1 = (f32[2048,64]{0,1:T(8,128)S(1)}, f32[2048,64]{0,1:T(8,128)}, u32[]{:S(2)}) copy-start(f32[2048,64]{0,1:T(8,128)} %param.8) | copy-start | bytes 1572868
  205.8 38.3 %copy-start.2 = (s32[2048,64]{0,1:T(8,128)S(1)}, s32[2048,64]{0,1:T(8,128)}, u32[]{:S(2)}) copy-start(s32[2048,64]{0,1:T(8,128)} %param.10) | copy-start | bytes 1572868
  247.6 249.7 %reduce-scatter.2.cloned.1.call-start = ((), (), s32[]{:S(2)}) async-start(), calls=%async_computation.2 | async-start | bytes 8912896 | tf_op jit(solution)/shard_map/reduce_scatter | solution.py:86
  318.1 0.7 copy-start.5
  318.8 1.0 copy-start.3
  318.8 1.0 copy-start.4
Sparse Core Ops, SparseCore 0:
  247.7 6.4 all-gather.4
  318.3 178.9 reduce-scatter.1
where the time goes:
time: 509 us; the launch traced here: 507 us
  waiting for transfers between devices  181 us (36%)
  other arithmetic  128 us (25%)
  blocking collectives  115 us (23%)
  matrix products  34.9 us (7%)
  local copies, waits for them, and re-layouts  33.7 us (7%)
  between operations  14.2 us (3%)
    reduce_scatter x1, waiting for transfers between devices, per_device(): lax.psum_scatter(histogram(owned_columns, weight_matrix).reshape(lax.axis...  176 us
    another operation x9, other arithmetic  118 us
    all_gather x1, blocking collectives, per_device(): lax.all_gather(risk_total[None, :], 'rows', axis=0, tiled=True)  42.2 us
    all_gather x1, blocking collectives, per_device(): lax.all_gather(hazard_total[None, :], 'rows', axis=0, tiled=True)  37.3 us
    all_gather x1, blocking collectives, per_device(): lax.all_gather(square_total[None, :], 'rows', axis=0, tiled=True)  35.3 us
    dot_general x4, matrix products, hist_step(): lax.dot_general(onehot, weight_rows, (((0,), (0,)), ((), ())), preferred_...  34.9 us
    reshape x2, local copies, waits for them, and re-layouts, per_device(): histogram(owned_columns, weight_matrix)  18.4 us
  transfers between devices with their start and end apart: 2, of which 2 were waited for; matrix products, arithmetic and copies ran while one was open for 1% of the time, Pallas kernels for 0%

commit v1 on v0

v1 whole, which is shorter than its diff:
```python
import functools

import jax
import jax.numpy as jnp
from jax import lax
from jax.experimental import pallas as pl
from jax.experimental.pallas import tpu as pltpu
from jax.sharding import PartitionSpec as P

BINS = 32
LEAVES = 2
MESH = pl.DeviceIdType.MESH
GROUP = 16
CODE = 32750.0 / (BINS * LEAVES * (1 + 1 / 32)) ** 0.25


def encode(x):
    size = jnp.maximum(jnp.abs(x), 1e-30)
    code = (lax.rsqrt(lax.rsqrt(size)) * CODE + 0.5).astype(jnp.int32)
    return jnp.where(x < 0, -code, code).astype(jnp.int16)


def decode(q):
    v = q.astype(jnp.int32).astype(jnp.float32) * (1.0 / CODE)
    return (v * v) * (v * jnp.abs(v))


def split_dot(tri, x):
    high = x.astype(jnp.bfloat16)
    low = (x - high.astype(jnp.float32)).astype(jnp.bfloat16)
    both = jnp.dot(tri, jnp.concatenate([high, low], axis=1), preferred_element_type=jnp.float32)
    return both[:, : x.shape[1]] + both[:, x.shape[1] :]


def kernel(
    R, U, score, event, leaf, bins, sf, sb,
    new_leaf, gout, hout,
    exp_s, risk_s, cum_s, bins_t, w_s, tile, gat, part, h1, r1, h2, r2, h3, r3, fin, sib,
    sA, rA, s1, q1, s2, q2, s3, q3, s4, q4,
):
    rows, EL = score.shape
    F = bins.shape[1]
    FPC = F // R
    UF = FPC // U
    UR = UF * BINS
    Z = R // 4
    HZ = Z * UR
    DP = GROUP // UF
    STEP = GROUP * BINS
    T = (R // 2) // DP
    TB = min(rows, 256)
    me = lax.axis_index("rows")
    c = lax.axis_index("feat")

    barrier = pltpu.get_barrier_semaphore()

    @pl.loop(1, R)
    def _(k):
        pl.semaphore_signal(barrier, inc=1, device_id={"rows": lax.rem(me + k, R)}, device_id_type=MESH)

    pl.semaphore_signal(barrier, inc=1, device_id={"feat": 1 - c}, device_id_type=MESH)

    ri = lax.broadcasted_iota(jnp.int32, (TB, TB), 0)
    ci = lax.broadcasted_iota(jnp.int32, (TB, TB), 1)
    low_half = lax.broadcasted_iota(jnp.int32, (TB, 2 * EL), 1) < EL

    def twice(x):
        return jnp.concatenate([x, x], axis=1)

    upper = jnp.where(ci >= ri, 1.0, 0.0).astype(jnp.bfloat16)
    carry = jnp.zeros((1, 2 * EL), jnp.float32)
    for b in reversed(range(rows // TB)):
        at = slice(b * TB, (b + 1) * TB)
        e = jnp.exp(twice(score[at, :]))
        exp_s[at, :] = e
        suffix = split_dot(upper, e) + carry
        risk_s[at, :] = suffix
        carry = suffix[0:1, :]
    tile[0] = jnp.broadcast_to(carry, (8, 2 * EL))

    pl.semaphore_wait(barrier, R)

    def total_copy(phase, k):
        return pltpu.make_async_remote_copy(
            src_ref=tile.at[phase], dst_ref=gat.at[phase, k - 1],
            send_sem=sA.at[phase, k - 1], recv_sem=rA.at[phase, k - 1],
            device_id={"rows": lax.rem(me + k, R)}, device_id_type=MESH,
        )

    @pl.loop(1, R)
    def _(k):
        total_copy(0, k).start()

    bins_t[...] = bins[...].astype(jnp.float32).T
    pick = jnp.where(lax.broadcasted_iota(jnp.int32, (F, EL), 0) == sf[...], 1.0, 0.0).astype(jnp.bfloat16)
    value = jnp.dot(
        bins[...].astype(jnp.float32).astype(jnp.bfloat16), pick, preferred_element_type=jnp.float32
    )
    new_leaf[...] = 2 * leaf[...] + jnp.where(value > sb[...].astype(jnp.float32), 1, 0)

    def gathered(phase, later):
        @pl.loop(1, R)
        def _(k):
            total_copy(phase, k).wait()

        def add(k, acc):
            wanted = (k > me) if later else (k <= me)
            return acc + jnp.where(wanted, gat[phase, k - 1], 0.0)

        return lax.fori_loop(1, R, add, jnp.zeros((8, 2 * EL), jnp.float32))[0:1, :]

    later_sum = gathered(0, True)

    lower = jnp.where(ci <= ri, 1.0, 0.0).astype(jnp.bfloat16)
    carry = jnp.zeros((1, 2 * EL), jnp.float32)
    for b in range(rows // TB):
        at = slice(b * TB, (b + 1) * TB)
        risk = risk_s[at, :] + later_sum
        share = twice(event[at, :]).astype(jnp.float32) / risk
        share = jnp.where(low_half, share, share / risk)
        prefix = split_dot(lower, share) + carry
        cum_s[at, :] = prefix
        carry = prefix[TB - 1 : TB, :]
    tile[1] = jnp.broadcast_to(carry, (8, 2 * EL))

    @pl.loop(1, R)
    def _(k):
        total_copy(1, k).start()

    earlier_sum = gathered(1, False)
    scale = BINS * LEAVES / (rows * R)
    for b in range(rows // TB):
        at = slice(b * TB, (b + 1) * TB)
        e = exp_s[at, :]
        p = e * (cum_s[at, :] + earlier_sum)
        p = jnp.where(low_half, p, e * p)
        turned = pltpu.roll(p, EL, 1)
        ev = twice(event[at, :]).astype(jnp.float32)
        grad_hess = scale * jnp.where(low_half, p - ev, turned - p)
        leaves = twice(leaf[at, :])
        for l in range(LEAVES):
            w_s[at, l * 2 * EL : (l + 1) * 2 * EL] = jnp.where(leaves == l, grad_hess, 0.0).astype(jnp.bfloat16)

    level = lax.broadcasted_iota(jnp.int32, (BINS, rows), 0).astype(jnp.float32).astype(jnp.bfloat16)

    def digits(u):
        par = lax.rem(u, 2)
        w1, w2 = 1 + par, 2 - par
        m1 = lax.rem(me // w1, 2)
        m2 = lax.rem(me // w2, 2)
        return w1, w2, m1, m2, me + w1 * (1 - 2 * m1), me + w2 * (1 - 2 * m2)

    def hist(u, t, d1, w1, w2):
        pieces = []
        for i in range(DP):
            spot = t * DP + i
            chip = 4 * lax.rem(spot, Z) + w2 * (spot // Z) + w1 * d1
            for j in range(UF):
                row = bins_t[pl.ds(chip * FPC + u * UF + j, 1), :].astype(jnp.bfloat16)
                hit = jnp.broadcast_to(row, (BINS, rows)) == level
                pieces.append(jnp.where(hit, jnp.bfloat16(1), jnp.bfloat16(0)))
        return jnp.dot(jnp.concatenate(pieces, axis=0), w_s[...], preferred_element_type=jnp.float32)

    def copy1(u):
        p1 = digits(u)[4]
        return pltpu.make_async_remote_copy(
            src_ref=h1.at[u], dst_ref=r1.at[u], send_sem=s1.at[u], recv_sem=q1.at[u],
            device_id={"rows": p1}, device_id_type=MESH,
        )

    def copy2(u):
        p2 = digits(u)[5]
        return pltpu.make_async_remote_copy(
            src_ref=h2.at[u], dst_ref=r2.at[u], send_sem=s2.at[u], recv_sem=q2.at[u],
            device_id={"rows": p2}, device_id_type=MESH,
        )

    mz = me // 4

    def copy3(u, k):
        return pltpu.make_async_remote_copy(
            src_ref=h3.at[u, k - 1], dst_ref=r3.at[u, k - 1],
            send_sem=s3.at[u, k - 1], recv_sem=q3.at[u, k - 1],
            device_id={"rows": 4 * lax.rem(mz + k, Z) + lax.rem(me, 4)}, device_id_type=MESH,
        )

    @pl.loop(0, U)
    def _(u):
        w1, w2, m1, *_ = digits(u)

        @pl.loop(0, T)
        def _(t):
            h1[u, pl.ds(pl.multiple_of(t * STEP, STEP), STEP), :] = encode(hist(u, t, 1 - m1, w1, w2))

        copy1(u).start()

    @pl.loop(0, U)
    def _(u):
        w1, w2, m1, *_ = digits(u)

        @pl.loop(0, T)
        def _(t):
            part[u, pl.ds(pl.multiple_of(t * STEP, STEP), STEP), :] = hist(u, t, m1, w1, w2)

    def second(u):
        m2 = digits(u)[3]
        copy1(u).wait_recv()
        away = pl.ds(pl.multiple_of((1 - m2) * HZ, HZ), HZ)
        h2[u] = encode(part[u, away, :] + decode(r1[u, away, :]))
        copy2(u).start()

    def third(u):
        m2 = digits(u)[3]
        copy2(u).wait_recv()

        def sums(z):
            near = pl.ds(pl.multiple_of(m2 * HZ + z * UR, UR), UR)
            there = pl.ds(pl.multiple_of(z * UR, UR), UR)
            return part[u, near, :] + decode(r1[u, near, :]) + decode(r2[u, there, :])

        @pl.loop(1, Z)
        def _(k):
            h3[u, k - 1] = encode(sums(lax.rem(mz + k, Z)))
            copy3(u, k).start()

        fin[u] = sums(mz)

    lag = min(2, U)

    @pl.loop(0, U + lag)
    def _(t):
        @pl.when(t < U)
        def _():
            second(t)

        @pl.when(t >= lag)
        def _():
            third(t - lag)

    @pl.loop(0, U)
    def _(u):
        @pl.loop(1, Z)
        def _(k):
            copy3(u, k).wait_recv()
            fin[u] = fin[u] + decode(r3[u, k - 1])

    half = U // 2
    swap = pltpu.make_async_remote_copy(
        src_ref=fin.at[pl.ds((1 - c) * half, half)], dst_ref=sib, send_sem=s4, recv_sem=q4,
        device_id={"feat": 1 - c}, device_id_type=MESH,
    )
    swap.start()

    @pl.loop(0, U)
    def _(u):
        copy1(u).wait_send()
        copy2(u).wait_send()

        @pl.loop(1, Z)
        def _(k):
            copy3(u, k).wait_send()

    swap.wait()
    lanes = lax.broadcasted_iota(jnp.int32, (UR, 2 * EL), 1) < EL
    for v in range(half):
        at = slice(v * UR, (v + 1) * UR)
        own, other = fin[c * half + v], sib[v]
        first = jnp.where(c == 0, own, other)
        last = jnp.where(c == 0, other, own)
        for l in range(LEAVES):
            a, z = (y[:, l * 2 * EL : (l + 1) * 2 * EL] for y in (first, last))
            gout[at, l, :] = jnp.where(lanes, a, pltpu.roll(z, EL, 1))
            hout[at, l, :] = jnp.where(lanes, pltpu.roll(a, EL, 1), z)


def per_device(R, score, event, leaf, bins, split_feature, split_bin):
    rows, EL = score.shape
    F = bins.shape[1]
    FPC = F // R
    U = min(8, FPC)
    UR = FPC // U * BINS
    Z = R // 4
    C = LEAVES * 2 * EL
    own = FPC // 2 * BINS
    f32, i16 = jnp.float32, jnp.int16
    dma = pltpu.SemaphoreType.DMA
    new_leaf, grad, hess = pl.pallas_call(
        functools.partial(kernel, R, U),
        out_shape=(
            jax.ShapeDtypeStruct((rows, EL), jnp.int32),
            jax.ShapeDtypeStruct((own, LEAVES, 2 * EL), f32),
            jax.ShapeDtypeStruct((own, LEAVES, 2 * EL), f32),
        ),
        in_specs=[pl.BlockSpec(memory_space=pltpu.VMEM)] * 6,
        out_specs=[pl.BlockSpec(memory_space=pltpu.VMEM)] * 3,
        scratch_shapes=[
            pltpu.VMEM((rows, 2 * EL), f32),
            pltpu.VMEM((rows, 2 * EL), f32),
            pltpu.VMEM((rows, 2 * EL), f32),
            pltpu.VMEM((F, rows), f32),
            pltpu.VMEM((rows, C), jnp.bfloat16),
            pltpu.VMEM((2, 8, 2 * EL), f32),
            pltpu.VMEM((2, R - 1, 8, 2 * EL), f32),
            pltpu.VMEM((U, R // 2 * UR, C), f32),
            pltpu.VMEM((U, R // 2 * UR, C), i16),
            pltpu.VMEM((U, R // 2 * UR, C), i16),
            pltpu.VMEM((U, Z * UR, C), i16),
            pltpu.VMEM((U, Z * UR, C), i16),
            pltpu.VMEM((U, Z - 1, UR, C), i16),
            pltpu.VMEM((U, Z - 1, UR, C), i16),
            pltpu.VMEM((U, UR, C), f32),
            pltpu.VMEM((U // 2, UR, C), f32),
            dma((2, R - 1)), dma((2, R - 1)),
            dma((U,)), dma((U,)), dma((U,)), dma((U,)),
            dma((U, Z - 1)), dma((U, Z - 1)),
            dma, dma,
        ],
        compiler_params=pltpu.CompilerParams(
            collective_id=0, has_side_effects=True, vmem_limit_bytes=52 * 2**20
        ),
        cost_estimate=pl.CostEstimate(
            flops=2 * F * BINS * rows * C, bytes_accessed=4 * rows * F, transcendentals=rows * EL
        ),
    )(score, event, leaf, bins, split_feature[None, :], split_bin[None, :])
    shape = (own // BINS, BINS, LEAVES, 2 * EL)
    return grad.reshape(shape), hess.reshape(shape), new_leaf


def solution(mesh):
    return jax.shard_map(
        functools.partial(per_device, mesh.shape["rows"]),
        mesh=mesh,
        in_specs=(
            P("rows", "feat"),
            P("rows", "feat"),
            P("rows", "feat"),
            P("rows", None),
            P("feat"),
            P("feat"),
        ),
        out_specs=(
            P(("rows", "feat"), None, None, None),
            P(("rows", "feat"), None, None, None),
            P("rows", "feat"),
        ),
        check_vma=False,
    )
```

time: 509 us -> 80.9 us (0.16)
  waiting for transfers between devices: 181 us -> 0 us
  other arithmetic: 128 us -> 0 us
  blocking collectives: 115 us -> 0 us
  Pallas kernels: 0 us -> 71.4 us
  matrix products: 34.9 us -> 0 us
  local copies, waits for them, and re-layouts: 33.7 us -> 8.67 us
  between operations: 14.2 us -> 0.67 us
    reduce_scatter x1 -> x0, waiting for transfers between devices: 176 us -> none  [per_device(): lax.psum_scatter(histogram(owned_columns, weight_matrix).reshape(lax.axis...]
    another operation x11 -> x0, other arithmetic: 120 us -> none
    all_gather x3 -> x0, blocking collectives: 115 us -> none  [the longest x1 42.2 us: per_device(): lax.all_gather(risk_total[None, :], 'rows', axis=0, tiled=True)]
    pallas_call x0 -> x1, Pallas kernels: none -> 71.4 us  [per_device(): pl.pallas_call(functools.partial(kernel, R, U), out_shape=(jax.ShapeDtype...]
    dot_general x4 -> x0, matrix products: 34.9 us -> none  [hist_step(): lax.dot_general(onehot, weight_rows, (((0,), (0,)), ((), ())), preferred_...]
    reshape x3 -> x0, local copies, waits for them, and re-layouts: 18.5 us -> none  [the longest x2 18.4 us: per_device(): histogram(owned_columns, weight_matrix)]
    eq x4 -> x0, other arithmetic: 5.99 us -> none  [hist_step(): column_piece[:, :, None] == levels]
  transfers between devices with their start and end apart: 2 -> 0, of which waited for: 2 -> 0; matrix products, arithmetic and copies ran while one was open for 1% -> 0% of each run, Pallas kernels for 0% -> 0%
where the time goes in v1:
time: 80.9 us; the launch traced here: 80.7 us
  Pallas kernels  71.4 us (88%)
  local copies, waits for them, and re-layouts  8.67 us (11%)
    pallas_call x1, Pallas kernels, per_device(): pl.pallas_call(functools.partial(kernel, R, U), out_shape=(jax.ShapeDtype...  71.4 us
    unnamed x12, local copies, waits for them, and re-layouts  8.67 us

profile of v1, /device:TPU:0, one launch (start us, length us, event | category | flops | bytes accessed | tf_op | source)
XLA Modules:
  0.0 80.7 jit_solution(14038586036998048701)
XLA Ops:
  0.6 0.0 copy-start.2
  0.6 0.0 copy-start
  0.7 0.0 copy-start.1
  0.7 2.4 %copy.9.score = f32[2048,64]{1,0:T(8,128)} copy(f32[2048,64]{0,1:T(8,128)} %param.6) | data formatting | bytes 1048576 | tf_op args[0]
  3.1 2.4 %copy.10.event = s32[2048,64]{1,0:T(8,128)} copy(s32[2048,64]{0,1:T(8,128)} %param.7) | data formatting | bytes 1048576 | tf_op args[1]
  5.5 0.0 copy-done.2
  5.5 1.3 %copy.11.leaf = s32[2048,64]{1,0:T(8,128)} copy(s32[2048,64]{0,1:T(8,128)S(1)} %copy-done.2) | data formatting | bytes 1048576 | tf_op args[2]
  6.8 0.0 copy-done
  6.8 0.0 copy-done.1
  6.8 71.4 %shard_map.85 = (s32[2048,64]{1,0:T(8,128)S(1)}, f32[256,2,128]{2,1,0:T(2,128)S(1)}, f32[256,2,128]{2,1,0:T(2,128)S(1)}) custom-call(f32[2048,64]{1,0:T(8,128)} %copy.9.score, s32[2048,64]{1,0:T(8,128)} %copy.10.event, s32[2048,64]{1,0:T(8,128)} %copy.11.leaf, s32[2048,256]{1,0:T(8,128)} %bins.1, s32[1,64]{1,0:T(1,128)S(1)} %bitcast.6, s32[1,64]{1,0:T(1,128)S(1)} %bitcast.7), custom_call_target="tpu_custom_call" | custom-call | flops 8589934592 | bytes 2097152 | tf_op jit(solution)/shard_map/pallas_call | solution.py:287
  78.2 1.1 %copy.12 = s32[2048,64]{0,1:T(8,128)} copy(s32[2048,64]{1,0:T(8,128)S(1)} %get-tuple-element.11) | data formatting | bytes 1048576
  79.3 0.7 copy.15
  80.0 0.7 copy.16
Async XLA Ops:
  0.6 4.8 %copy-start.2 = (s32[2048,64]{0,1:T(8,128)S(1)}, s32[2048,64]{0,1:T(8,128)}, u32[]{:S(2)}) copy-start(s32[2048,64]{0,1:T(8,128)} %param.8) | copy-start | bytes 1572868
  0.6 6.2 %copy-start = (s32[64]{0:T(128)S(1)}, s32[64]{0:T(128)}, u32[]{:S(2)}) copy-start(s32[64]{0:T(128)} %param.10) | copy-start | bytes 772
  0.7 6.2 %copy-start.1 = (s32[64]{0:T(128)S(1)}, s32[64]{0:T(128)}, u32[]{:S(2)}) copy-start(s32[64]{0:T(128)} %param.11) | copy-start | bytes 772

commit v2 on v1

--- a/solution.py
+++ b/solution.py
@@ -35,10 +35,10 @@
 def kernel(
     R, U, score, event, leaf, bins, sf, sb,
     new_leaf, gout, hout,
-    exp_s, risk_s, cum_s, bins_t, w_s, tile, gat, part, h1, r1, h2, r2, h3, r3, fin, sib,
+    exp_s, risk_s, cum_s, event_s, leaf_s, bins_t, w_s, tile, gat, part, h1, r1, h2, r2, h3, r3, fin, sib,
     sA, rA, s1, q1, s2, q2, s3, q3, s4, q4,
 ):
-    rows, EL = score.shape
+    EL, rows = score.shape
     F = bins.shape[1]
     FPC = F // R
     UF = FPC // U
@@ -65,13 +65,13 @@
     low_half = lax.broadcasted_iota(jnp.int32, (TB, 2 * EL), 1) < EL
 
     def twice(x):
-        return jnp.concatenate([x, x], axis=1)
+        return jnp.concatenate([x, x], axis=0).T
 
     upper = jnp.where(ci >= ri, 1.0, 0.0).astype(jnp.bfloat16)
     carry = jnp.zeros((1, 2 * EL), jnp.float32)
     for b in reversed(range(rows // TB)):
         at = slice(b * TB, (b + 1) * TB)
-        e = jnp.exp(twice(score[at, :]))
+        e = jnp.exp(twice(score[:, at]))
         exp_s[at, :] = e
         suffix = split_dot(upper, e) + carry
         risk_s[at, :] = suffix
@@ -91,12 +91,10 @@
     def _(k):
         total_copy(0, k).start()
 
-    bins_t[...] = bins[...].astype(jnp.float32).T
-    pick = jnp.where(lax.broadcasted_iota(jnp.int32, (F, EL), 0) == sf[...], 1.0, 0.0).astype(jnp.bfloat16)
-    value = jnp.dot(
-        bins[...].astype(jnp.float32).astype(jnp.bfloat16), pick, preferred_element_type=jnp.float32
-    )
-    new_leaf[...] = 2 * leaf[...] + jnp.where(value > sb[...].astype(jnp.float32), 1, 0)
+    for b in range(rows // TB):
+        at = slice(b * TB, (b + 1) * TB)
+        event_s[at, :] = twice(event[:, at].astype(jnp.float32))
+        leaf_s[at, :] = twice(leaf[:, at].astype(jnp.float32))
 
     def gathered(phase, later):
         @pl.loop(1, R)
@@ -116,7 +114,7 @@
     for b in range(rows // TB):
         at = slice(b * TB, (b + 1) * TB)
         risk = risk_s[at, :] + later_sum
-        share = twice(event[at, :]).astype(jnp.float32) / risk
+        share = event_s[at, :] / risk
         share = jnp.where(low_half, share, share / risk)
         prefix = split_dot(lower, share) + carry
         cum_s[at, :] = prefix
@@ -126,6 +124,14 @@
     @pl.loop(1, R)
     def _(k):
         total_copy(1, k).start()
+
+    bins_t[...] = bins[...].astype(jnp.float32).T
+    ids = lax.broadcasted_iota(jnp.int32, (EL, F), 1).astype(jnp.float32)
+    wanted = jnp.broadcast_to(sf[...].astype(jnp.float32), (F, EL)).T
+    pick = jnp.where(ids == wanted, 1.0, 0.0).astype(jnp.bfloat16)
+    limit = jnp.broadcast_to(sb[...].astype(jnp.float32), (F, EL)).T[:, 0:1]
+    value = jnp.dot(pick, bins_t[...].astype(jnp.bfloat16), preferred_element_type=jnp.float32)
+    new_leaf[...] = 2 * leaf[...] + jnp.where(value > limit, 1, 0)
 
     earlier_sum = gathered(1, False)
     scale = BINS * LEAVES / (rows * R)
@@ -135,9 +141,9 @@
         p = e * (cum_s[at, :] + earlier_sum)
         p = jnp.where(low_half, p, e * p)
         turned = pltpu.roll(p, EL, 1)
-        ev = twice(event[at, :]).astype(jnp.float32)
+        ev = event_s[at, :]
         grad_hess = scale * jnp.where(low_half, p - ev, turned - p)
-        leaves = twice(leaf[at, :])
+        leaves = leaf_s[at, :]
         for l in range(LEAVES):
             w_s[at, l * 2 * EL : (l + 1) * 2 * EL] = jnp.where(leaves == l, grad_hess, 0.0).astype(jnp.bfloat16)
 
@@ -184,8 +190,7 @@
             device_id={"rows": 4 * lax.rem(mz + k, Z) + lax.rem(me, 4)}, device_id_type=MESH,
         )
 
-    @pl.loop(0, U)
-    def _(u):
+    def first(u):
         w1, w2, m1, *_ = digits(u)
 
         @pl.loop(0, T)
@@ -194,8 +199,7 @@
 
         copy1(u).start()
 
-    @pl.loop(0, U)
-    def _(u):
+    def keep(u):
         w1, w2, m1, *_ = digits(u)
 
         @pl.loop(0, T)
@@ -225,17 +229,23 @@
 
         fin[u] = sums(mz)
 
-    lag = min(2, U)
-
-    @pl.loop(0, U + lag)
+    lag = min(4, U)
+    lag3 = lag + 2
+
+    @pl.loop(0, U + lag3)
     def _(t):
         @pl.when(t < U)
         def _():
-            second(t)
-
-        @pl.when(t >= lag)
+            first(t)
+
+        @pl.when((t >= lag) & (t < U + lag))
         def _():
-            third(t - lag)
+            keep(t - lag)
+            second(t - lag)
+
+        @pl.when(t >= lag3)
+        def _():
+            third(t - lag3)
 
     @pl.loop(0, U)
     def _(u):
@@ -287,13 +297,15 @@
     new_leaf, grad, hess = pl.pallas_call(
         functools.partial(kernel, R, U),
         out_shape=(
-            jax.ShapeDtypeStruct((rows, EL), jnp.int32),
+            jax.ShapeDtypeStruct((EL, rows), jnp.int32),
             jax.ShapeDtypeStruct((own, LEAVES, 2 * EL), f32),
             jax.ShapeDtypeStruct((own, LEAVES, 2 * EL), f32),
         ),
         in_specs=[pl.BlockSpec(memory_space=pltpu.VMEM)] * 6,
         out_specs=[pl.BlockSpec(memory_space=pltpu.VMEM)] * 3,
         scratch_shapes=[
+            pltpu.VMEM((rows, 2 * EL), f32),
+            pltpu.VMEM((rows, 2 * EL), f32),
             pltpu.VMEM((rows, 2 * EL), f32),
             pltpu.VMEM((rows, 2 * EL), f32),
             pltpu.VMEM((rows, 2 * EL), f32),
@@ -321,9 +333,9 @@
         cost_estimate=pl.CostEstimate(
             flops=2 * F * BINS * rows * C, bytes_accessed=4 * rows * F, transcendentals=rows * EL
         ),
-    )(score, event, leaf, bins, split_feature[None, :], split_bin[None, :])
+    )(score.T, event.T, leaf.T, bins, split_feature[None, :], split_bin[None, :])
     shape = (own // BINS, BINS, LEAVES, 2 * EL)
-    return grad.reshape(shape), hess.reshape(shape), new_leaf
+    return grad.reshape(shape), hess.reshape(shape), new_leaf.T
 
 
 def solution(mesh):

time: 80.9 us -> 71.3 us (0.88)
  Pallas kernels: 71.4 us -> 65.9 us
  local copies, waits for them, and re-layouts: 8.67 us -> 4.54 us
    pallas_call x1, Pallas kernels: 71.4 us -> 65.9 us  [per_device(): pl.pallas_call(functools.partial(kernel, R, U), out_shape=(jax.ShapeDtype...]
    unnamed x12 -> x9, local copies, waits for them, and re-layouts: 8.67 us -> 4.54 us
where the time goes in v2:
time: 71.3 us; the launch traced here: 71.1 us
  Pallas kernels  65.9 us (92%)
  local copies, waits for them, and re-layouts  4.54 us (6%)
    pallas_call x1, Pallas kernels, per_device(): pl.pallas_call(functools.partial(kernel, R, U), out_shape=(jax.ShapeDtype...  65.9 us
    unnamed x9, local copies, waits for them, and re-layouts  4.54 us

profile of v2, /device:TPU:0, one launch (start us, length us, event | category | flops | bytes accessed | tf_op | source)
XLA Modules:
  0.0 71.1 jit_solution(11289401255525832382)
XLA Ops:
  0.6 0.0 copy-start
  0.6 1.0 %copy-done = f32[2048,64]{0,1:T(8,128)S(1)} copy-done((f32[2048,64]{0,1:T(8,128)S(1)}, f32[2048,64]{0,1:T(8,128)}, u32[]{:S(2)}) %copy-start) | copy-done | bytes 524312
  1.7 0.0 copy-start.1
  1.7 0.7 copy-done.1
  2.3 0.0 copy-start.2
  2.3 0.7 copy-done.2
  3.0 65.9 %shard_map.85 = (s32[64,2048]{1,0:T(8,128)S(1)}, f32[256,2,128]{2,1,0:T(2,128)S(1)}, f32[256,2,128]{2,1,0:T(2,128)S(1)}) custom-call(f32[64,2048]{1,0:T(8,128)S(1)} %bitcast.11, s32[64,2048]{1,0:T(8,128)} %bitcast.14, s32[64,2048]{1,0:T(8,128)} %bitcast.15, s32[2048,256]{1,0:T(8,128)} %bins.1, s32[1,64]{1,0:T(1,128)S(1)} %bitcast.12, s32[1,64]{1,0:T(1,128)S(1)} %bitcast.13), custom_call_target="tpu_custom_call" | custom-call | flops 8589934592 | bytes 2097152 | tf_op jit(solution)/shard_map/pallas_call | solution.py:297
  68.9 0.7 copy.12
  69.6 0.7 copy.13
  70.3 0.8 %copy.14 = s32[2048,64]{0,1:T(8,128)} copy(s32[2048,64]{0,1:T(8,128)S(1)} %bitcast.8) | data formatting | bytes 1048576
Async XLA Ops:
  0.6 1.0 %copy-start = (f32[2048,64]{0,1:T(8,128)S(1)}, f32[2048,64]{0,1:T(8,128)}, u32[]{:S(2)}) copy-start(f32[2048,64]{0,1:T(8,128)} %param.6) | copy-start | bytes 1572868
  1.7 0.7 copy-start.1
  2.3 0.7 copy-start.2

commit v3 on v2

--- a/solution.py
+++ b/solution.py
@@ -99,7 +99,7 @@
     def gathered(phase, later):
         @pl.loop(1, R)
         def _(k):
-            total_copy(phase, k).wait()
+            total_copy(phase, k).wait_recv()
 
         def add(k, acc):
             wanted = (k > me) if later else (k <= me)
@@ -126,12 +126,6 @@
         total_copy(1, k).start()
 
     bins_t[...] = bins[...].astype(jnp.float32).T
-    ids = lax.broadcasted_iota(jnp.int32, (EL, F), 1).astype(jnp.float32)
-    wanted = jnp.broadcast_to(sf[...].astype(jnp.float32), (F, EL)).T
-    pick = jnp.where(ids == wanted, 1.0, 0.0).astype(jnp.bfloat16)
-    limit = jnp.broadcast_to(sb[...].astype(jnp.float32), (F, EL)).T[:, 0:1]
-    value = jnp.dot(pick, bins_t[...].astype(jnp.bfloat16), preferred_element_type=jnp.float32)
-    new_leaf[...] = 2 * leaf[...] + jnp.where(value > limit, 1, 0)
 
     earlier_sum = gathered(1, False)
     scale = BINS * LEAVES / (rows * R)
@@ -229,7 +223,7 @@
 
         fin[u] = sums(mz)
 
-    lag = min(4, U)
+    lag = min(2, U)
     lag3 = lag + 2
 
     @pl.loop(0, U + lag3)
@@ -246,6 +240,13 @@
         @pl.when(t >= lag3)
         def _():
             third(t - lag3)
+
+    ids = lax.broadcasted_iota(jnp.int32, (EL, F), 1).astype(jnp.float32)
+    wanted = jnp.broadcast_to(sf[...].astype(jnp.float32), (F, EL)).T
+    pick = jnp.where(ids == wanted, 1.0, 0.0).astype(jnp.bfloat16)
+    limit = jnp.broadcast_to(sb[...].astype(jnp.float32), (F, EL)).T[:, 0:1]
+    value = jnp.dot(pick, bins_t[...].astype(jnp.bfloat16), preferred_element_type=jnp.float32)
+    new_leaf[...] = 2 * leaf[...] + jnp.where(value > limit, 1, 0)
 
     @pl.loop(0, U)
     def _(u):
@@ -269,6 +270,11 @@
         @pl.loop(1, Z)
         def _(k):
             copy3(u, k).wait_send()
+
+    @pl.loop(1, R)
+    def _(k):
+        total_copy(0, k).wait_send()
+        total_copy(1, k).wait_send()
 
     swap.wait()
     lanes = lax.broadcasted_iota(jnp.int32, (UR, 2 * EL), 1) < EL

time: 71.3 us -> 69 us (0.968)
  Pallas kernels: 65.9 us -> 63.6 us
    pallas_call x1, Pallas kernels: 65.9 us -> 63.6 us  [per_device(): pl.pallas_call(functools.partial(kernel, R, U), out_shape=(jax.ShapeDtype...]
where the time goes in v3:
time: 69 us; the launch traced here: 68.8 us
  Pallas kernels  63.6 us (92%)
  local copies, waits for them, and re-layouts  4.54 us (7%)
    pallas_call x1, Pallas kernels, per_device(): pl.pallas_call(functools.partial(kernel, R, U), out_shape=(jax.ShapeDtype...  63.6 us
    unnamed x9, local copies, waits for them, and re-layouts  4.54 us

profile of v3, /device:TPU:0, one launch (start us, length us, event | category | flops | bytes accessed | tf_op | source)
XLA Modules:
  0.0 68.8 jit_solution(13236943050630127525)
XLA Ops:
  0.6 0.0 copy-start
  0.6 1.0 %copy-done = f32[2048,64]{0,1:T(8,128)S(1)} copy-done((f32[2048,64]{0,1:T(8,128)S(1)}, f32[2048,64]{0,1:T(8,128)}, u32[]{:S(2)}) %copy-start) | copy-done | bytes 524312
  1.7 0.0 copy-start.1
  1.7 0.7 copy-done.1
  2.3 0.0 copy-start.2
  2.3 0.7 copy-done.2
  3.0 63.6 %shard_map.85 = (s32[64,2048]{1,0:T(8,128)S(1)}, f32[256,2,128]{2,1,0:T(2,128)S(1)}, f32[256,2,128]{2,1,0:T(2,128)S(1)}) custom-call(f32[64,2048]{1,0:T(8,128)S(1)} %bitcast.11, s32[64,2048]{1,0:T(8,128)} %bitcast.14, s32[64,2048]{1,0:T(8,128)} %bitcast.15, s32[2048,256]{1,0:T(8,128)} %bins.1, s32[1,64]{1,0:T(1,128)S(1)} %bitcast.12, s32[1,64]{1,0:T(1,128)S(1)} %bitcast.13), custom_call_target="tpu_custom_call" | custom-call | flops 8589934592 | bytes 2097152 | tf_op jit(solution)/shard_map/pallas_call | solution.py:303
  66.6 0.7 %copy.12 = f32[8,32,2,128]{3,2,1,0:T(2,128)} copy(f32[8,32,2,128]{3,2,1,0:T(2,128)S(1)} %bitcast.10) | data formatting | bytes 524288
  67.3 0.7 %copy.13 = f32[8,32,2,128]{3,2,1,0:T(2,128)} copy(f32[8,32,2,128]{3,2,1,0:T(2,128)S(1)} %bitcast.9) | data formatting | bytes 524288
  68.0 0.8 %copy.14 = s32[2048,64]{0,1:T(8,128)} copy(s32[2048,64]{0,1:T(8,128)S(1)} %bitcast.8) | data formatting | bytes 1048576
Async XLA Ops:
  0.6 1.0 %copy-start = (f32[2048,64]{0,1:T(8,128)S(1)}, f32[2048,64]{0,1:T(8,128)}, u32[]{:S(2)}) copy-start(f32[2048,64]{0,1:T(8,128)} %param.6) | copy-start | bytes 1572868
  1.7 0.7 copy-start.1
  2.3 0.7 copy-start.2
